TPU v7x, 32 devices: a whole 2x2x4 slice. The times are simulated.
32 devices in a mesh: group: 2 (over x), atom: 4 (over y, core), layer: 4 (over z).
Axes of the slice: x: 2, y: 2, z: 4, core: 2. Of those that a mesh axis runs over, the one named last changes fastest.
Arguments:
- activations: bfloat16 [256, 4, 2304], P('group', 'layer'), parts along dimension 0, may hold values from -6 to 6
- encoder: bfloat16 [8, 2304, 16384], P(('group', 'layer'), None, 'atom'), parts along dimension 0, may hold values from -0.0625 to 0.0625
- decoder: bfloat16 [32768, 4, 2304], P(('group', 'atom'), 'layer'), parts along dimension 0, may hold values from -1 to 1
- thresholds: float32 [32768], P(('group', 'atom')), parts along dimension 0, may hold values from 0.05 to 0.8
Outputs:
- codes: bfloat16 [256, 16384], P('group', 'atom'), parts along dimension 0
- reconstruction: bfloat16 [256, 4, 2304], P(('group', 'atom'), 'layer'), parts along dimension 0
There are 2 independent parts, one for each index of `group`. A program takes and returns all parts, laid end to end along the dimension named above; each array names one. Nothing has to cross between parts.
All inputs are finite; a program needn't handle non-finite values.
Results may differ from a plain program's by a relative error of at most 0.02.
The roundings to bfloat16 on the way count: a program that leaves them out, or rounds other values in their place, can miss the bound.
Values may be sent and summed in bfloat16 or wider, within the bound.
A program may use at most 128 MiB of HBM per device.

v0:
```python
import jax
import jax.numpy as jnp
from jax import lax
from jax.sharding import PartitionSpec as P

REFINES = 2
step_rate = 0.15
learn_rate = 0.001


def shards(activations, encoder, decoder, thresholds):
    rows_in = activations[:, 0, :]
    enc_local = encoder[0]
    dec_local = decoder[:, 0, :]
    tokens = rows_in.shape[0]
    atom_devices = lax.axis_size("atom")

    def spread(code_state):
        return code_state.astype(jnp.bfloat16)

    def residual_of(coded_now, weights):
        row_count = tokens // atom_devices
        partial_value = lax.psum_scatter(
            jnp.dot(coded_now, weights, preferred_element_type=jnp.float32).astype(jnp.bfloat16),
            "atom",
            scatter_dimension=0,
            tiled=True,
        ).astype(jnp.float32)
        own_rows = lax.dynamic_slice_in_dim(
            rows_in, lax.axis_index("atom") * row_count, row_count, 0
        ).astype(jnp.float32)
        residual = lax.all_gather(
            (own_rows - partial_value).astype(jnp.bfloat16), "atom", axis=0, tiled=True
        )
        return (residual, False)

    def refine(code_state, coded_now, weights):
        residual, transposed = residual_of(coded_now, weights)
        gradient = lax.psum(
            lax.dot_general(
                residual, weights, (((1,), (1,)), ((), ())), preferred_element_type=jnp.float32
            ).astype(jnp.bfloat16),
            "layer",
        ).astype(jnp.float32)
        code_state = jax.nn.relu(code_state + step_rate * gradient - step_rate * thresholds)
        return (code_state, spread(code_state))

    preact = lax.psum(
        jnp.dot(rows_in, enc_local, preferred_element_type=jnp.float32).astype(jnp.bfloat16),
        "layer",
    ).astype(jnp.float32)
    code_state = jax.nn.relu(preact - thresholds)
    coded_now = spread(code_state)
    for sweep in range(REFINES):
        code_state, coded_now = refine(code_state, coded_now, dec_local)
    residual, transposed = residual_of(coded_now, dec_local)
    update = lax.dot_general(
        coded_now, residual, (((0,), (0,)), ((), ())), preferred_element_type=jnp.float32
    )
    renewed = (dec_local.astype(jnp.float32) + learn_rate * (update / tokens)).astype(jnp.bfloat16)
    code_state, coded_now = refine(code_state, coded_now, renewed)
    rebuilt = lax.psum_scatter(
        jnp.dot(coded_now, renewed, preferred_element_type=jnp.float32).astype(jnp.bfloat16),
        "atom",
        scatter_dimension=0,
        tiled=True,
    )
    reconstruction = rebuilt[:, None, :]
    return (coded_now, reconstruction)


def solution(mesh):
    return jax.shard_map(
        shards,
        mesh=mesh,
        in_specs=(
            P("group", "layer", None),
            P(("group", "layer"), None, "atom"),
            P(("group", "atom"), "layer", None),
            P(("group", "atom")),
        ),
        out_specs=(P("group", "atom"), P(("group", "atom"), "layer", None)),
        check_vma=False,
    )
```

profile of v0, /device:TPU:0, one launch (start us, length us, event | category | flops | bytes accessed | tf_op | source)
XLA Modules:
  0.0 487.0 jit_solution(16662554394716441295)
XLA Ops:
  7.2 0.0 copy-start.4
  7.2 0.0 all-reduce.5.cloned.1.call-start
  7.2 10.2 %fusion.12 = bf16[128,4096]{1,0:T(8,128)(2,1)} fusion(bf16[1,2304,4096]{2,1,0:T(8,128)(2,1)} %param.5, bf16[128,1,2304]{2,0,1:T(8,128)(2,1)} %param.4), kind=kOutput, calls=%fused_computation.13 | convolution fusion | flops 2416443392 | bytes 20512768 | tf_op jit(solution)/shard_map/dot_general | solution.py:49
  17.4 0.0 all-reduce.5.cloned.1.call-update
  17.4 0.0 copy-start.3
  17.4 0.0 reduce-scatter.6.cloned.1.call-start
  17.5 54.6 %all-reduce.5.cloned.1.call-done = bf16[128,4096]{1,0:T(8,128)(2,1)} async-done(((bf16[128,4096]{1,0:T(8,128)(2,1)}), bf16[128,4096]{1,0:T(8,128)(2,1)}) %all-reduce.5.cloned.1.call-update) | async-done | bytes 1048592 | tf_op jit(solution)/shard_map/psum | solution.py:48
  72.1 0.0 copy-done.4
  72.1 10.1 %fusion.21 = bf16[128,2304]{1,0:T(8,128)(2,1)} fusion(bf16[4096,1,2304]{2,0,1:T(8,128)(2,1)} %param.6, bf16[128,4096]{1,0:T(8,128)(2,1)} %all-reduce.5.cloned.1.call-done, f32[4096]{0:T(1024)S(1)} %copy-done.4), kind=kOutput, calls=%fused_computation.17 | convolution fusion | flops 2418311168 | bytes 20529152 | tf_op jit(solution)/shard_map/dot_general | solution.py:24
  82.2 0.0 reduce-scatter.6.cloned.1.call-update
  82.3 0.0 all-reduce.7.cloned.1.call-start
  82.3 21.6 %reduce-scatter.6.cloned.1.call-done = bf16[32,2304]{1,0:T(8,128)(2,1)} async-done(((bf16[128,2304]{1,0:T(8,128)(2,1)}), bf16[32,2304]{1,0:T(8,128)(2,1)}) %reduce-scatter.6.cloned.1.call-update) | async-done | bytes 147472 | tf_op jit(solution)/shard_map/reduce_scatter | solution.py:23
  103.9 0.0 copy-done.3
  103.9 0.9 fusion.42
  104.8 7.1 %all_gather.12 = bf16[128,2304]{1,0:T(8,128)(2,1)S(1)} all-gather(bf16[32,2304]{1,0:T(8,128)(2,1)S(1)} %fusion.42), channel_id=1, replica_groups=mesh['group'=2,'atom'=4,'layer'=4] {'atom'}, dimensions={0}, use_global_device_ids=true | all-gather | bytes 737280 | tf_op jit(solution)/shard_map/all_gather | solution.py:32
  112.0 0.0 copy-start
  112.0 13.6 %fusion.15 = bf16[128,4096]{1,0:T(8,128)(2,1)} fusion(bf16[128,2304]{1,0:T(8,128)(2,1)S(1)} %all_gather.12, bf16[4096,1,2304]{2,0,1:T(8,128)(2,1)} %param.6), kind=kOutput, calls=%fused_computation.14 | convolution fusion | flops 2416443392 | bytes 20512768 | tf_op jit(solution)/shard_map/dot_general | solution.py:40
  125.5 0.0 all-reduce.7.cloned.1.call-update
  125.5 0.0 reduce-scatter.8.cloned.1.call-start
  125.6 52.3 %all-reduce.7.cloned.1.call-done = bf16[128,4096]{1,0:T(8,128)(2,1)} async-done(((bf16[128,4096]{1,0:T(8,128)(2,1)}), bf16[128,4096]{1,0:T(8,128)(2,1)}) %all-reduce.7.cloned.1.call-update) | async-done | bytes 1048592 | tf_op jit(solution)/shard_map/psum | solution.py:39
  177.9 0.0 copy-done
  177.9 10.4 %fusion.24 = bf16[128,2304]{1,0:T(8,128)(2,1)} fusion(bf16[4096,1,2304]{2,0,1:T(8,128)(2,1)} %param.6, bf16[128,4096]{1,0:T(8,128)(2,1)} %all-reduce.7.cloned.1.call-done, bf16[128,4096]{1,0:T(8,128)(2,1)S(1)} %copy-done, f32[4096]{0:T(1024)S(1)} %broadcast_multiply_fusion, f32[4096]{0:T(1024)S(1)} %copy-done.4), kind=kOutput, calls=%fused_computation.18 | convolution fusion | flops 2420932608 | bytes 21594112 | tf_op jit(solution)/shard_map/dot_general | solution.py:24
  188.3 0.0 reduce-scatter.8.cloned.1.call-update
  188.3 0.0 all-reduce.9.cloned.1.call-start
  188.4 21.5 %reduce-scatter.8.cloned.1.call-done = bf16[32,2304]{1,0:T(8,128)(2,1)} async-done(((bf16[128,2304]{1,0:T(8,128)(2,1)}), bf16[32,2304]{1,0:T(8,128)(2,1)}) %reduce-scatter.8.cloned.1.call-update) | async-done | bytes 147472 | tf_op jit(solution)/shard_map/reduce_scatter | solution.py:23
  209.9 0.9 fusion.43
  210.9 7.3 %all_gather.13 = bf16[128,2304]{1,0:T(8,128)(2,1)S(1)} all-gather(bf16[32,2304]{1,0:T(8,128)(2,1)S(1)} %fusion.43), channel_id=1, replica_groups=mesh['group'=2,'atom'=4,'layer'=4] {'atom'}, dimensions={0}, use_global_device_ids=true | all-gather | bytes 737280 | tf_op jit(solution)/shard_map/all_gather | solution.py:32
  218.2 0.0 copy-start.2
  218.2 13.6 %fusion.18 = bf16[128,4096]{1,0:T(8,128)(2,1)} fusion(bf16[128,2304]{1,0:T(8,128)(2,1)S(1)} %all_gather.13, bf16[4096,1,2304]{2,0,1:T(8,128)(2,1)} %param.6), kind=kOutput, calls=%fused_computation.15 | convolution fusion | flops 2416443392 | bytes 20512768 | tf_op jit(solution)/shard_map/dot_general | solution.py:40
  231.8 0.0 all-reduce.9.cloned.1.call-update
  231.8 0.0 reduce-scatter.10.cloned.1.call-start
  231.8 52.3 %all-reduce.9.cloned.1.call-done = bf16[128,4096]{1,0:T(8,128)(2,1)} async-done(((bf16[128,4096]{1,0:T(8,128)(2,1)}), bf16[128,4096]{1,0:T(8,128)(2,1)}) %all-reduce.9.cloned.1.call-update) | async-done | bytes 1048592 | tf_op jit(solution)/shard_map/psum | solution.py:39
  284.2 0.0 copy-done.2
  284.2 2.1 fusion.41
  286.3 9.8 %fusion.27 = bf16[128,2304]{1,0:T(8,128)(2,1)} fusion(bf16[128,4096]{1,0:T(8,128)(2,1)S(1)} %fusion.41, bf16[4096,1,2304]{2,0,1:T(8,128)(2,1)} %param.6), kind=kOutput, calls=%fused_computation.19 | convolution fusion | flops 2416214016 | bytes 20512768 | tf_op jit(solution)/shard_map/dot_general | solution.py:24
  296.1 0.0 reduce-scatter.10.cloned.1.call-update
  296.1 0.0 reduce-scatter.12.cloned.1.call-start
  296.2 21.6 %reduce-scatter.10.cloned.1.call-done = bf16[32,2304]{1,0:T(8,128)(2,1)} async-done(((bf16[128,2304]{1,0:T(8,128)(2,1)}), bf16[32,2304]{1,0:T(8,128)(2,1)}) %reduce-scatter.10.cloned.1.call-update) | async-done | bytes 147472 | tf_op jit(solution)/shard_map/reduce_scatter | solution.py:23
  317.8 1.0 fusion.44
  318.8 7.8 %all_gather.14 = bf16[128,2304]{1,0:T(8,128)(2,1)} all-gather(bf16[32,2304]{1,0:T(8,128)(2,1)S(1)} %fusion.44), channel_id=1, replica_groups=mesh['group'=2,'atom'=4,'layer'=4] {'atom'}, dimensions={0}, use_global_device_ids=true | all-gather | bytes 737280 | tf_op jit(solution)/shard_map/all_gather | solution.py:32
  326.6 12.9 %add_convert_fusion = bf16[4096,2304]{1,0:T(8,128)(2,1)} fusion(bf16[128,4096]{1,0:T(8,128)(2,1)S(1)} %fusion.41, bf16[128,2304]{1,0:T(8,128)(2,1)} %all_gather.14, bf16[4096,1,2304]{2,0,1:T(8,128)(2,1)} %param.6), kind=kOutput, calls=%fused_computation | convolution fusion | flops 2453667840 | bytes 39387136 | tf_op jit(solution)/shard_map/dot_general | solution.py:57
  339.4 9.8 %convolution_convert_fusion.2 = bf16[128,2304]{1,0:T(8,128)(2,1)} fusion(bf16[128,4096]{1,0:T(8,128)(2,1)S(1)} %fusion.41, bf16[4096,2304]{1,0:T(8,128)(2,1)} %add_convert_fusion), kind=kOutput, calls=%fused_computation.21 | convolution fusion | flops 2416214016 | bytes 20512768 | tf_op jit(solution)/shard_map/dot_general | solution.py:24
  349.2 0.0 reduce-scatter.12.cloned.1.call-update
  349.3 0.0 all-reduce.11.cloned.1.call-start
  349.3 22.6 %reduce-scatter.12.cloned.1.call-done = bf16[32,2304]{1,0:T(8,128)(2,1)} async-done(((bf16[128,2304]{1,0:T(8,128)(2,1)}), bf16[32,2304]{1,0:T(8,128)(2,1)}) %reduce-scatter.12.cloned.1.call-update) | async-done | bytes 147472 | tf_op jit(solution)/shard_map/reduce_scatter | solution.py:23
  371.9 1.0 fusion.45
  372.9 7.1 %all_gather.15 = bf16[128,2304]{1,0:T(8,128)(2,1)S(1)} all-gather(bf16[32,2304]{1,0:T(8,128)(2,1)S(1)} %fusion.45), channel_id=1, replica_groups=mesh['group'=2,'atom'=4,'layer'=4] {'atom'}, dimensions={0}, use_global_device_ids=true | all-gather | bytes 737280 | tf_op jit(solution)/shard_map/all_gather | solution.py:32
  380.0 13.5 %convolution_convert_fusion = bf16[128,4096]{1,0:T(8,128)(2,1)} fusion(bf16[128,2304]{1,0:T(8,128)(2,1)S(1)} %all_gather.15, bf16[4096,2304]{1,0:T(8,128)(2,1)} %add_convert_fusion), kind=kOutput, calls=%fused_computation.16 | convolution fusion | flops 2416443392 | bytes 20512768 | tf_op jit(solution)/shard_map/dot_general | solution.py:40
  393.5 0.0 all-reduce.11.cloned.1.call-update
  393.5 0.3 reduce-scatter.14.cloned.1.call-start
  393.8 52.0 %all-reduce.11.cloned.1.call-done = bf16[128,4096]{1,0:T(8,128)(2,1)} async-done(((bf16[128,4096]{1,0:T(8,128)(2,1)}), bf16[128,4096]{1,0:T(8,128)(2,1)}) %all-reduce.11.cloned.1.call-update) | async-done | bytes 1048592 | tf_op jit(solution)/shard_map/psum | solution.py:39
  445.9 2.8 maximum_convert_fusion
  448.7 0.0 copy-start.1
  448.7 10.2 %convolution_convert_fusion.1 = bf16[128,2304]{1,0:T(8,128)(2,1)} fusion(bf16[128,4096]{1,0:T(8,128)(2,1)S(1)} %maximum_convert_fusion, bf16[4096,2304]{1,0:T(8,128)(2,1)} %add_convert_fusion), kind=kOutput, calls=%fused_computation.20 | convolution fusion | flops 2416214016 | bytes 20512768 | tf_op jit(solution)/shard_map/dot_general | solution.py:63
  458.9 0.0 copy-done.1
  458.9 0.0 reduce-scatter.14.cloned.1.call-update
  458.9 21.6 %reduce-scatter.14.cloned.1.call-done = bf16[32,2304]{1,0:T(8,128)(2,1)} async-done(((bf16[128,2304]{1,0:T(8,128)(2,1)}), bf16[32,2304]{1,0:T(8,128)(2,1)}) %reduce-scatter.14.cloned.1.call-update) | async-done | bytes 147472 | tf_op jit(solution)/shard_map/reduce_scatter | solution.py:62
  (1 shorter events, 0.0 us)
Async XLA Ops:
  7.2 64.9 %copy-start.4 = (f32[4096]{0:T(1024)S(1)}, f32[4096]{0:T(1024)}, u32[]{:S(2)}) copy-start(f32[4096]{0:T(1024)} %param.7) | copy-start | bytes 49156
  7.2 64.9 %all-reduce.5.cloned.1.call-start = ((), (), s32[]{:S(2)}) async-start(), calls=%async_computation.5 | async-start | bytes 2097152 | tf_op jit(solution)/shard_map/psum | solution.py:48
  17.4 86.5 %copy-start.3 = (bf16[128,1,2304]{2,0,1:T(8,128)(2,1)S(1)}, bf16[128,1,2304]{2,0,1:T(8,128)(2,1)}, u32[]{:S(2)}) copy-start(bf16[128,1,2304]{2,0,1:T(8,128)(2,1)} %param.4) | copy-start | bytes 1769476
  17.4 86.5 %reduce-scatter.6.cloned.1.call-start = ((), (), s32[]{:S(2)}) async-start(), calls=%async_computation.6 | async-start | bytes 737280 | tf_op jit(solution)/shard_map/reduce_scatter | solution.py:23
  82.3 95.6 %all-reduce.7.cloned.1.call-start = ((), (), s32[]{:S(2)}) async-start(), calls=%async_computation.7 | async-start | bytes 2097152 | tf_op jit(solution)/shard_map/psum | solution.py:39
  112.0 65.9 %copy-start = (bf16[128,4096]{1,0:T(8,128)(2,1)S(1)}, bf16[128,4096]{1,0:T(8,128)(2,1)}, u32[]{:S(2)}) copy-start(bf16[128,4096]{1,0:T(8,128)(2,1)} %all-reduce.5.cloned.1.call-done) | copy-start | bytes 3145732
  125.5 84.4 %reduce-scatter.8.cloned.1.call-start = ((), (), s32[]{:S(2)}) async-start(), calls=%async_computation.8 | async-start | bytes 737280 | tf_op jit(solution)/shard_map/reduce_scatter | solution.py:23
  188.3 95.8 %all-reduce.9.cloned.1.call-start = ((), (), s32[]{:S(2)}) async-start(), calls=%async_computation.9 | async-start | bytes 2097152 | tf_op jit(solution)/shard_map/psum | solution.py:39
  218.2 65.9 %copy-start.2 = (bf16[128,4096]{1,0:T(8,128)(2,1)S(1)}, bf16[128,4096]{1,0:T(8,128)(2,1)}, u32[]{:S(2)}) copy-start(bf16[128,4096]{1,0:T(8,128)(2,1)} %all-reduce.7.cloned.1.call-done) | copy-start | bytes 3145732
  231.8 86.0 %reduce-scatter.10.cloned.1.call-start = ((), (), s32[]{:S(2)}) async-start(), calls=%async_computation.10 | async-start | bytes 737280 | tf_op jit(solution)/shard_map/reduce_scatter | solution.py:23
  296.1 75.8 %reduce-scatter.12.cloned.1.call-start = ((), (), s32[]{:S(2)}) async-start(), calls=%async_computation.11 | async-start | bytes 737280 | tf_op jit(solution)/shard_map/reduce_scatter | solution.py:23
  349.3 96.6 %all-reduce.11.cloned.1.call-start = ((), (), s32[]{:S(2)}) async-start(), calls=%async_computation.12 | async-start | bytes 2097152 | tf_op jit(solution)/shard_map/psum | solution.py:39
  393.5 87.0 %reduce-scatter.14.cloned.1.call-start = ((), (), s32[]{:S(2)}) async-start(), calls=%async_computation.13 | async-start | bytes 737280 | tf_op jit(solution)/shard_map/reduce_scatter | solution.py:62
  448.7 10.2 %copy-start.1 = (bf16[128,4096]{1,0:T(8,128)(2,1)}, bf16[128,4096]{1,0:T(8,128)(2,1)S(1)}, u32[]{:S(2)}) copy-start(bf16[128,4096]{1,0:T(8,128)(2,1)S(1)} %maximum_convert_fusion) | copy-start | bytes 3145732
Sparse Core Ops, SparseCore 0:
  17.5 54.5 all-reduce.4
  82.4 21.4 reduce-scatter.5
  125.7 52.1 all-reduce.6
  188.5 21.4 reduce-scatter.7
  231.9 52.1 all-reduce.8
  296.2 21.4 reduce-scatter.9
  349.4 22.4 reduce-scatter.11
  393.6 52.1 all-reduce.10
  459.0 21.4 reduce-scatter.13
where the time goes:
time: 488 us; the launch traced here: 487 us
  waiting for transfers between devices  320 us (66%)
  matrix products  114 us (23%)
  blocking collectives  29.4 us (6%)
  between operations  13.9 us (3%)
  other arithmetic  8.87 us (2%)
    psum x3, waiting for transfers between devices, refine(): lax.psum(lax.dot_general(residual, weights, (((1,), (1,)), ((), ())), pre...  157 us
    reduce_scatter x4, waiting for transfers between devices, residual_of(): lax.psum_scatter(jnp.dot(coded_now, weights, preferred_element_type=jnp.f...  87.3 us
    psum x1, waiting for transfers between devices, shards(): lax.psum(jnp.dot(rows_in, enc_local, preferred_element_type=jnp.float32)....  54.6 us
    dot_general x3, matrix products, refine(): lax.dot_general(residual, weights, (((1,), (1,)), ((), ())), preferred_el...  40.6 us
    dot_general x4, matrix products, residual_of(): jnp.dot(coded_now, weights, preferred_element_type=jnp.float32)  40.2 us
    all_gather x4, blocking collectives, residual_of(): lax.all_gather((own_rows - partial_value).astype(jnp.bfloat16), 'atom', a...  29.4 us
    reduce_scatter x1, waiting for transfers between devices, shards(): lax.psum_scatter(jnp.dot(coded_now, renewed, preferred_element_type=jnp.f...  21.6 us
    dot_general x1, matrix products, shards(): lax.dot_general(coded_now, residual, (((0,), (0,)), ((), ())), preferred_...  12.9 us
  transfers between devices with their start and end apart: 9, of which 9 were waited for; matrix products, arithmetic and copies ran while one was open for 0% of the time, Pallas kernels for 0%

commit v1 on v0

--- a/solution.py
+++ b/solution.py
@@ -1,11 +1,20 @@
+import functools
 import jax
 import jax.numpy as jnp
 from jax import lax
 from jax.sharding import PartitionSpec as P
+from jax.lax import all_gather
 
 REFINES = 2
 step_rate = 0.15
 learn_rate = 0.001
+
+
+def lift_digits(panel, group_axis):
+    return all_gather(panel, group_axis).sum(axis=0)
+
+
+lift_core_by_axis = functools.partial(lift_digits, group_axis="layer")
 
 
 def shards(activations, encoder, decoder, thresholds):
@@ -45,9 +54,8 @@
         code_state = jax.nn.relu(code_state + step_rate * gradient - step_rate * thresholds)
         return (code_state, spread(code_state))
 
-    preact = lax.psum(
-        jnp.dot(rows_in, enc_local, preferred_element_type=jnp.float32).astype(jnp.bfloat16),
-        "layer",
+    preact = lift_core_by_axis(
+        jnp.dot(rows_in, enc_local, preferred_element_type=jnp.float32).astype(jnp.bfloat16)
     ).astype(jnp.float32)
     code_state = jax.nn.relu(preact - thresholds)
     coded_now = spread(code_state)

time: 488 us -> 518 us (1.061)
  waiting for transfers between devices: 320 us -> 348 us
    all_gather x0 -> x1, waiting for transfers between devices: none -> 83.6 us  [lift_digits(): return all_gather(panel, group_axis).sum(axis=0)]
    psum x1 -> x0, waiting for transfers between devices: 54.6 us -> none  [shards(): lax.psum(jnp.dot(rows_in, enc_local, preferred_element_type=jnp.float32)....]
where the time goes in v1:
time: 518 us
  waiting for transfers between devices  348 us (67%)
  matrix products  114 us (22%)
  blocking collectives  29.2 us (6%)
  between operations  13.9 us (3%)
  other arithmetic  11.9 us (2%)
    psum x3, waiting for transfers between devices, refine(): lax.psum(lax.dot_general(residual, weights, (((1,), (1,)), ((), ())), pre...  156 us
    reduce_scatter x4, waiting for transfers between devices, residual_of(): lax.psum_scatter(jnp.dot(coded_now, weights, preferred_element_type=jnp.f...  86.3 us
    all_gather x1, waiting for transfers between devices, lift_digits(): return all_gather(panel, group_axis).sum(axis=0)  83.6 us
    dot_general x3, matrix products, refine(): lax.dot_general(residual, weights, (((1,), (1,)), ((), ())), preferred_el...  40.5 us
    dot_general x4, matrix products, residual_of(): jnp.dot(coded_now, weights, preferred_element_type=jnp.float32)  39.9 us
    all_gather x4, blocking collectives, residual_of(): lax.all_gather((own_rows - partial_value).astype(jnp.bfloat16), 'atom', a...  29.2 us
    reduce_scatter x1, waiting for transfers between devices, shards(): lax.psum_scatter(jnp.dot(coded_now, renewed, preferred_element_type=jnp.f...  21.6 us
    dot_general x1, matrix products, shards(): lax.dot_general(coded_now, residual, (((0,), (0,)), ((), ())), preferred_...  12.9 us
  transfers between devices with their start and end apart: 9, of which 9 were waited for; matrix products, arithmetic and copies ran while one was open for 0% of the time, Pallas kernels for 0%

profile of v1, /device:TPU:0, one launch (start us, length us, event | category | flops | bytes accessed | tf_op | source)
XLA Modules:
  0.0 517.7 jit_solution(11319858499886546206)
XLA Ops:
  7.2 0.0 all-gather.3.cloned.1.call-start
  7.2 10.2 %fusion.12 = bf16[128,4096]{1,0:T(8,128)(2,1)} fusion(bf16[1,2304,4096]{2,1,0:T(8,128)(2,1)} %param.5, bf16[128,1,2304]{2,0,1:T(8,128)(2,1)} %param.4), kind=kOutput, calls=%fused_computation.13 | convolution fusion | flops 2416443392 | bytes 20512768 | tf_op jit(solution)/shard_map/dot_general | solution.py:58
  17.4 0.0 all-gather.3.cloned.1.call-update
  17.4 0.0 reduce-scatter.6.cloned.1.call-start
  17.4 83.6 %all-gather.3.cloned.1.call-done = bf16[512,4096]{1,0:T(8,128)(2,1)} async-done(((bf16[128,4096]{1,0:T(8,128)(2,1)}), bf16[512,4096]{1,0:T(8,128)(2,1)}) %all-gather.3.cloned.1.call-update) | async-done | bytes 4194320 | tf_op jit(solution)/shard_map/all_gather | solution.py:14
  101.0 0.0 copy-start.3
  101.0 3.1 reduce_sum.12
  104.1 0.0 copy-done.3
  104.1 0.0 copy-start.2
  104.1 9.9 %fusion.21 = bf16[128,2304]{1,0:T(8,128)(2,1)} fusion(bf16[4096,1,2304]{2,0,1:T(8,128)(2,1)} %param.6, bf16[128,4096]{1,0:T(8,128)(2,1)S(1)} %reduce_sum.12, f32[4096]{0:T(1024)S(1)} %copy-done.3), kind=kOutput, calls=%fused_computation.17 | convolution fusion | flops 2418311168 | bytes 20529152 | tf_op jit(solution)/shard_map/dot_general | solution.py:33
  114.0 0.0 reduce-scatter.6.cloned.1.call-update
  114.0 0.0 all-reduce.4.cloned.1.call-start
  114.1 20.7 %reduce-scatter.6.cloned.1.call-done = bf16[32,2304]{1,0:T(8,128)(2,1)} async-done(((bf16[128,2304]{1,0:T(8,128)(2,1)}), bf16[32,2304]{1,0:T(8,128)(2,1)}) %reduce-scatter.6.cloned.1.call-update) | async-done | bytes 147472 | tf_op jit(solution)/shard_map/reduce_scatter | solution.py:32
  134.8 0.0 copy-done.2
  134.8 0.9 fusion.42
  135.7 7.1 %all_gather.20 = bf16[128,2304]{1,0:T(8,128)(2,1)S(1)} all-gather(bf16[32,2304]{1,0:T(8,128)(2,1)S(1)} %fusion.42), channel_id=1, replica_groups=mesh['group'=2,'atom'=4,'layer'=4] {'atom'}, dimensions={0}, use_global_device_ids=true | all-gather | bytes 737280 | tf_op jit(solution)/shard_map/all_gather | solution.py:41
  142.9 13.4 %fusion.15 = bf16[128,4096]{1,0:T(8,128)(2,1)} fusion(bf16[128,2304]{1,0:T(8,128)(2,1)S(1)} %all_gather.20, bf16[4096,1,2304]{2,0,1:T(8,128)(2,1)} %param.6), kind=kOutput, calls=%fused_computation.14 | convolution fusion | flops 2416443392 | bytes 20512768 | tf_op jit(solution)/shard_map/dot_general | solution.py:49
  156.3 0.0 all-reduce.4.cloned.1.call-update
  156.3 0.2 reduce-scatter.8.cloned.1.call-start
  156.6 52.1 %all-reduce.4.cloned.1.call-done = bf16[128,4096]{1,0:T(8,128)(2,1)} async-done(((bf16[128,4096]{1,0:T(8,128)(2,1)}), bf16[128,4096]{1,0:T(8,128)(2,1)}) %all-reduce.4.cloned.1.call-update) | async-done | bytes 1048592 | tf_op jit(solution)/shard_map/psum | solution.py:48
  208.7 10.4 %fusion.24 = bf16[128,2304]{1,0:T(8,128)(2,1)} fusion(bf16[4096,1,2304]{2,0,1:T(8,128)(2,1)} %param.6, bf16[128,4096]{1,0:T(8,128)(2,1)} %all-reduce.4.cloned.1.call-done, bf16[128,4096]{1,0:T(8,128)(2,1)S(1)} %reduce_sum.12, f32[4096]{0:T(1024)S(1)} %broadcast_multiply_fusion, f32[4096]{0:T(1024)S(1)} %copy-done.3), kind=kOutput, calls=%fused_computation.18 | convolution fusion | flops 2420932608 | bytes 21594112 | tf_op jit(solution)/shard_map/dot_general | solution.py:33
  219.1 0.0 reduce-scatter.8.cloned.1.call-update
  219.2 0.0 all-reduce.6.cloned.1.call-start
  219.2 21.6 %reduce-scatter.8.cloned.1.call-done = bf16[32,2304]{1,0:T(8,128)(2,1)} async-done(((bf16[128,2304]{1,0:T(8,128)(2,1)}), bf16[32,2304]{1,0:T(8,128)(2,1)}) %reduce-scatter.8.cloned.1.call-update) | async-done | bytes 147472 | tf_op jit(solution)/shard_map/reduce_scatter | solution.py:32
  240.8 0.9 fusion.43
  241.7 7.1 %all_gather.21 = bf16[128,2304]{1,0:T(8,128)(2,1)S(1)} all-gather(bf16[32,2304]{1,0:T(8,128)(2,1)S(1)} %fusion.43), channel_id=1, replica_groups=mesh['group'=2,'atom'=4,'layer'=4] {'atom'}, dimensions={0}, use_global_device_ids=true | all-gather | bytes 737280 | tf_op jit(solution)/shard_map/all_gather | solution.py:41
  248.8 0.0 copy-start.1
  248.9 13.6 %fusion.18 = bf16[128,4096]{1,0:T(8,128)(2,1)} fusion(bf16[128,2304]{1,0:T(8,128)(2,1)S(1)} %all_gather.21, bf16[4096,1,2304]{2,0,1:T(8,128)(2,1)} %param.6), kind=kOutput, calls=%fused_computation.15 | convolution fusion | flops 2416443392 | bytes 20512768 | tf_op jit(solution)/shard_map/dot_general | solution.py:49
  262.4 0.0 all-reduce.6.cloned.1.call-update
  262.4 0.0 reduce-scatter.10.cloned.1.call-start
  262.5 52.3 %all-reduce.6.cloned.1.call-done = bf16[128,4096]{1,0:T(8,128)(2,1)} async-done(((bf16[128,4096]{1,0:T(8,128)(2,1)}), bf16[128,4096]{1,0:T(8,128)(2,1)}) %all-reduce.6.cloned.1.call-update) | async-done | bytes 1048592 | tf_op jit(solution)/shard_map/psum | solution.py:48
  314.8 0.0 copy-done.1
  314.8 2.1 fusion.41
  316.9 9.8 %fusion.27 = bf16[128,2304]{1,0:T(8,128)(2,1)} fusion(bf16[128,4096]{1,0:T(8,128)(2,1)S(1)} %fusion.41, bf16[4096,1,2304]{2,0,1:T(8,128)(2,1)} %param.6), kind=kOutput, calls=%fused_computation.19 | convolution fusion | flops 2416214016 | bytes 20512768 | tf_op jit(solution)/shard_map/dot_general | solution.py:33
  326.7 0.0 reduce-scatter.10.cloned.1.call-update
  326.8 0.0 reduce-scatter.12.cloned.1.call-start
  326.8 21.5 %reduce-scatter.10.cloned.1.call-done = bf16[32,2304]{1,0:T(8,128)(2,1)} async-done(((bf16[128,2304]{1,0:T(8,128)(2,1)}), bf16[32,2304]{1,0:T(8,128)(2,1)}) %reduce-scatter.10.cloned.1.call-update) | async-done | bytes 147472 | tf_op jit(solution)/shard_map/reduce_scatter | solution.py:32
  348.4 1.0 fusion.44
  349.4 7.8 %all_gather.22 = bf16[128,2304]{1,0:T(8,128)(2,1)} all-gather(bf16[32,2304]{1,0:T(8,128)(2,1)S(1)} %fusion.44), channel_id=1, replica_groups=mesh['group'=2,'atom'=4,'layer'=4] {'atom'}, dimensions={0}, use_global_device_ids=true | all-gather | bytes 737280 | tf_op jit(solution)/shard_map/all_gather | solution.py:41
  357.2 12.9 %add_convert_fusion = bf16[4096,2304]{1,0:T(8,128)(2,1)} fusion(bf16[128,4096]{1,0:T(8,128)(2,1)S(1)} %fusion.41, bf16[128,2304]{1,0:T(8,128)(2,1)} %all_gather.22, bf16[4096,1,2304]{2,0,1:T(8,128)(2,1)} %param.6), kind=kOutput, calls=%fused_computation | convolution fusion | flops 2453667840 | bytes 39387136 | tf_op jit(solution)/shard_map/dot_general | solution.py:65
  370.1 9.8 %convolution_convert_fusion.2 = bf16[128,2304]{1,0:T(8,128)(2,1)} fusion(bf16[128,4096]{1,0:T(8,128)(2,1)S(1)} %fusion.41, bf16[4096,2304]{1,0:T(8,128)(2,1)} %add_convert_fusion), kind=kOutput, calls=%fused_computation.21 | convolution fusion | flops 2416214016 | bytes 20512768 | tf_op jit(solution)/shard_map/dot_general | solution.py:33
  379.9 0.0 reduce-scatter.12.cloned.1.call-update
  379.9 0.0 all-reduce.8.cloned.1.call-start
  379.9 22.5 %reduce-scatter.12.cloned.1.call-done = bf16[32,2304]{1,0:T(8,128)(2,1)} async-done(((bf16[128,2304]{1,0:T(8,128)(2,1)}), bf16[32,2304]{1,0:T(8,128)(2,1)}) %reduce-scatter.12.cloned.1.call-update) | async-done | bytes 147472 | tf_op jit(solution)/shard_map/reduce_scatter | solution.py:32
  402.5 1.0 fusion.45
  403.5 7.1 %all_gather.23 = bf16[128,2304]{1,0:T(8,128)(2,1)S(1)} all-gather(bf16[32,2304]{1,0:T(8,128)(2,1)S(1)} %fusion.45), channel_id=1, replica_groups=mesh['group'=2,'atom'=4,'layer'=4] {'atom'}, dimensions={0}, use_global_device_ids=true | all-gather | bytes 737280 | tf_op jit(solution)/shard_map/all_gather | solution.py:41
  410.6 13.5 %convolution_convert_fusion = bf16[128,4096]{1,0:T(8,128)(2,1)} fusion(bf16[128,2304]{1,0:T(8,128)(2,1)S(1)} %all_gather.23, bf16[4096,2304]{1,0:T(8,128)(2,1)} %add_convert_fusion), kind=kOutput, calls=%fused_computation.16 | convolution fusion | flops 2416443392 | bytes 20512768 | tf_op jit(solution)/shard_map/dot_general | solution.py:49
  424.1 0.0 all-reduce.8.cloned.1.call-update
  424.1 0.3 reduce-scatter.14.cloned.1.call-start
  424.4 52.0 %all-reduce.8.cloned.1.call-done = bf16[128,4096]{1,0:T(8,128)(2,1)} async-done(((bf16[128,4096]{1,0:T(8,128)(2,1)}), bf16[128,4096]{1,0:T(8,128)(2,1)}) %all-reduce.8.cloned.1.call-update) | async-done | bytes 1048592 | tf_op jit(solution)/shard_map/psum | solution.py:48
  476.5 2.8 maximum_convert_fusion
  479.3 0.0 copy-start
  479.3 10.2 %convolution_convert_fusion.1 = bf16[128,2304]{1,0:T(8,128)(2,1)} fusion(bf16[128,4096]{1,0:T(8,128)(2,1)S(1)} %maximum_convert_fusion, bf16[4096,2304]{1,0:T(8,128)(2,1)} %add_convert_fusion), kind=kOutput, calls=%fused_computation.20 | convolution fusion | flops 2416214016 | bytes 20512768 | tf_op jit(solution)/shard_map/dot_general | solution.py:71
  489.5 0.0 copy-done
  489.5 0.0 reduce-scatter.14.cloned.1.call-update
  489.5 21.6 %reduce-scatter.14.cloned.1.call-done = bf16[32,2304]{1,0:T(8,128)(2,1)} async-done(((bf16[128,2304]{1,0:T(8,128)(2,1)}), bf16[32,2304]{1,0:T(8,128)(2,1)}) %reduce-scatter.14.cloned.1.call-update) | async-done | bytes 147472 | tf_op jit(solution)/shard_map/reduce_scatter | solution.py:70
  (1 shorter events, 0.0 us)
Async XLA Ops:
  7.2 93.8 %all-gather.3.cloned.1.call-start = ((), (), s32[]{:S(2)}) async-start(), calls=%async_computation.13 | async-start | bytes 5242880 | tf_op jit(solution)/shard_map/all_gather | solution.py:14
  17.4 117.4 %reduce-scatter.6.cloned.1.call-start = ((), (), s32[]{:S(2)}) async-start(), calls=%async_computation.5 | async-start | bytes 737280 | tf_op jit(solution)/shard_map/reduce_scatter | solution.py:32
  101.0 3.1 copy-start.3
  104.1 30.7 %copy-start.2 = (bf16[128,1,2304]{2,0,1:T(8,128)(2,1)S(1)}, bf16[128,1,2304]{2,0,1:T(8,128)(2,1)}, u32[]{:S(2)}) copy-start(bf16[128,1,2304]{2,0,1:T(8,128)(2,1)} %param.4) | copy-start | bytes 1769476
  114.0 94.7 %all-reduce.4.cloned.1.call-start = ((), (), s32[]{:S(2)}) async-start(), calls=%async_computation.6 | async-start | bytes 2097152 | tf_op jit(solution)/shard_map/psum | solution.py:48
  156.3 84.4 %reduce-scatter.8.cloned.1.call-start = ((), (), s32[]{:S(2)}) async-start(), calls=%async_computation.7 | async-start | bytes 737280 | tf_op jit(solution)/shard_map/reduce_scatter | solution.py:32
  219.2 95.6 %all-reduce.6.cloned.1.call-start = ((), (), s32[]{:S(2)}) async-start(), calls=%async_computation.8 | async-start | bytes 2097152 | tf_op jit(solution)/shard_map/psum | solution.py:48
  248.8 65.9 %copy-start.1 = (bf16[128,4096]{1,0:T(8,128)(2,1)S(1)}, bf16[128,4096]{1,0:T(8,128)(2,1)}, u32[]{:S(2)}) copy-start(bf16[128,4096]{1,0:T(8,128)(2,1)} %all-reduce.4.cloned.1.call-done) | copy-start | bytes 3145732
  262.4 85.9 %reduce-scatter.10.cloned.1.call-start = ((), (), s32[]{:S(2)}) async-start(), calls=%async_computation.9 | async-start | bytes 737280 | tf_op jit(solution)/shard_map/reduce_scatter | solution.py:32
  326.8 75.7 %reduce-scatter.12.cloned.1.call-start = ((), (), s32[]{:S(2)}) async-start(), calls=%async_computation.10 | async-start | bytes 737280 | tf_op jit(solution)/shard_map/reduce_scatter | solution.py:32
  379.9 96.6 %all-reduce.8.cloned.1.call-start = ((), (), s32[]{:S(2)}) async-start(), calls=%async_computation.11 | async-start | bytes 2097152 | tf_op jit(solution)/shard_map/psum | solution.py:48
  424.1 87.0 %reduce-scatter.14.cloned.1.call-start = ((), (), s32[]{:S(2)}) async-start(), calls=%async_computation.12 | async-start | bytes 737280 | tf_op jit(solution)/shard_map/reduce_scatter | solution.py:70
  479.3 10.2 %copy-start = (bf16[128,4096]{1,0:T(8,128)(2,1)}, bf16[128,4096]{1,0:T(8,128)(2,1)S(1)}, u32[]{:S(2)}) copy-start(bf16[128,4096]{1,0:T(8,128)(2,1)S(1)} %maximum_convert_fusion) | copy-start | bytes 3145732
Sparse Core Ops, SparseCore 0:
  17.5 83.4 all-gather.2
  114.1 20.5 reduce-scatter.5
  156.5 52.2 all-reduce.3
  219.3 21.4 reduce-scatter.7
  262.6 52.1 all-reduce.5
  326.9 21.4 reduce-scatter.9
  380.0 22.4 reduce-scatter.11
  424.3 52.1 all-reduce.7
  489.6 21.4 reduce-scatter.13
